TPU v7x, 256 devices: a whole 4x4x8 slice. The times are simulated.
256 devices in a mesh: row: 16 (over z, core), col: 16 (over x, y).
Axes of the slice: x: 4, y: 4, z: 8, core: 2. Of those that a mesh axis runs over, the one named last changes fastest.
Arguments:
- activations: bfloat16 [2048, 16384], P('row', 'col'), may hold values from -0.26367188 to 0.26367188
- out_grad: bfloat16 [2048, 26624], P('col', 'row'), may hold values from -6 to 6
- weight: bfloat16 [16384, 26624], P('col', 'row'), may hold values from -0.046875 to 0.046875
Outputs:
- input_grad: bfloat16 [2048, 16384], P('row', 'col')
- weight_grad: bfloat16 [16384, 26624], P('col', 'row')
All inputs are finite; a program needn't handle non-finite values.
Results may differ from a plain program's by a relative error of at most 0.0012.
Values may be sent and summed in bfloat16 or wider, within the bound.
A program may use at most 128 MiB of HBM per device.

v0:
```python
import jax
import jax.numpy as jnp
from jax import lax
from jax.sharding import PartitionSpec as P


def per_device(activations, out_grad, weight):
    grad_rows = lax.all_gather(out_grad, "col", axis=0, tiled=True)
    picked = grad_rows
    summed = lax.dot_general(
        lax.all_gather(activations, "row", axis=0, tiled=True),
        picked,
        (((0,), (0,)), ((), ())),
        preferred_element_type=jnp.float32,
    )
    weight_grad = summed.astype(jnp.bfloat16)
    picked = grad_rows
    input_grad = lax.psum_scatter(
        lax.dot_general(
            picked, weight, (((1,), (1,)), ((), ())), preferred_element_type=jnp.float32
        ),
        "row",
        scatter_dimension=0,
        tiled=True,
    ).astype(jnp.bfloat16)
    return (input_grad, weight_grad)


def solution(mesh):
    placed = (P("row", "col"), P("col", "row"), P("col", "row"))
    return jax.shard_map(
        per_device,
        mesh=mesh,
        in_specs=placed,
        out_specs=(P("row", "col"), P("col", "row")),
        check_vma=False,
    )
```

profile of v0, /device:TPU:28, one launch (start us, length us, event | category | flops | bytes accessed | tf_op | source)
XLA Modules:
  0.0 205.6 jit_solution(11458869175665431134)
XLA Ops:
  7.2 0.0 copy-start
  7.2 0.0 all-gather.3.cloned.1.call-start
  7.2 0.7 all-gather.3.cloned.1.call-update
  7.9 0.0 all-gather.5.cloned.1.call-start
  8.0 0.7 all-gather.5.cloned.1.call-update
  8.7 0.0 reduce-scatter.2.cloned.1.call-start
  8.7 71.6 %all-gather.3.cloned.1.call-done = bf16[2048,1664]{1,0:T(8,128)(2,1)} async-done(((bf16[128,1664]{1,0:T(8,128)(2,1)}), bf16[2048,1664]{1,0:T(8,128)(2,1)}) %all-gather.3.cloned.1.call-update) | async-done | bytes 6815760 | tf_op jit(solution)/shard_map/all_gather | solution.py:8
  80.3 0.0 copy-done
  80.3 11.9 %fusion = f32[2048,1024]{1,0:T(8,128)} fusion(bf16[2048,1664]{1,0:T(8,128)(2,1)} %all-gather.3.cloned.1.call-done, bf16[1024,1664]{1,0:T(8,128)(2,1)S(1)} %copy-done), kind=kOutput, calls=%fused_computation.1 | convolution fusion | flops 6979321856 | bytes 18612224 | tf_op jit(solution)/shard_map/dot_general | solution.py:19
  92.2 0.0 reduce-scatter.2.cloned.1.call-update
  92.3 33.3 %all-gather.5.cloned.1.call-done = bf16[2048,1024]{1,0:T(8,128)(2,1)} async-done(((bf16[128,1024]{1,0:T(8,128)(2,1)}), bf16[2048,1024]{1,0:T(8,128)(2,1)}) %all-gather.5.cloned.1.call-update) | async-done | bytes 4194320 | tf_op jit(solution)/shard_map/all_gather | solution.py:11
  125.6 12.8 %convolution_convert_fusion = bf16[1024,1664]{1,0:T(8,128)(2,1)} fusion(bf16[2048,1024]{1,0:T(8,128)(2,1)} %all-gather.5.cloned.1.call-done, bf16[2048,1664]{1,0:T(8,128)(2,1)} %all-gather.3.cloned.1.call-done), kind=kOutput, calls=%fused_computation | convolution fusion | flops 6981025792 | bytes 14417920 | tf_op jit(solution)/shard_map/dot_general | solution.py:10
  138.4 58.9 %reduce-scatter.2.cloned.1.call-done = f32[128,1024]{1,0:T(8,128)} async-done(((f32[2048,1024]{1,0:T(8,128)}), f32[128,1024]{1,0:T(8,128)}) %reduce-scatter.2.cloned.1.call-update) | async-done | bytes 524304 | tf_op jit(solution)/shard_map/reduce_scatter | solution.py:18
  197.3 1.8 convert_element_type.6
Async XLA Ops:
  7.2 73.2 %copy-start = (bf16[1024,1664]{1,0:T(8,128)(2,1)S(1)}, bf16[1024,1664]{1,0:T(8,128)(2,1)}, u32[]{:S(2)}) copy-start(bf16[1024,1664]{1,0:T(8,128)(2,1)} %param.5) | copy-start | bytes 10223620
  7.2 73.1 %all-gather.3.cloned.1.call-start = ((), (), s32[]{:S(2)}) async-start(), calls=%async_computation.1 | async-start | bytes 7241728 | tf_op jit(solution)/shard_map/all_gather | solution.py:8
  7.9 117.7 %all-gather.5.cloned.1.call-start = ((), (), s32[]{:S(2)}) async-start(), calls=%async_computation.3 | async-start | bytes 4456448 | tf_op jit(solution)/shard_map/all_gather | solution.py:11
  8.7 188.6 %reduce-scatter.2.cloned.1.call-start = ((), (), s32[]{:S(2)}) async-start(), calls=%async_computation.2 | async-start | bytes 8912896 | tf_op jit(solution)/shard_map/reduce_scatter | solution.py:18
Sparse Core Ops, SparseCore 0:
  10.5 69.7 all-gather.2
  82.1 43.4 all-gather.4
  128.2 69.0 reduce-scatter.1
where the time goes:
time: 206 us
  waiting for transfers between devices  165 us (80%)
  matrix products  24.7 us (12%)
  between operations  13.8 us (7%)
    all_gather x1, waiting for transfers between devices, per_device(): grad_rows = lax.all_gather(out_grad, 'col', axis=0, tiled=True)  71.6 us
    reduce_scatter x1, waiting for transfers between devices, per_device(): lax.psum_scatter(lax.dot_general(picked, weight, (((1,), (1,)), ((), ()))...  58.9 us
    all_gather x1, waiting for transfers between devices, per_device(): lax.all_gather(activations, 'row', axis=0, tiled=True)  33.3 us
    dot_general x1, matrix products, per_device(): lax.dot_general(lax.all_gather(activations, 'row', axis=0, tiled=True), p...  12.8 us
    dot_general x1, matrix products, per_device(): lax.dot_general(picked, weight, (((1,), (1,)), ((), ())), preferred_eleme...  11.9 us
  transfers between devices with their start and end apart: 3, of which 3 were waited for; matrix products, arithmetic and copies ran while one was open for 12% of the time, Pallas kernels for 0%

commit v1 on v0

v1 whole, which is shorter than its diff:
```python
import functools

import jax
import jax.numpy as jnp
from jax import lax
from jax.experimental import pallas as pl
from jax.experimental.pallas import tpu as pltpu
from jax.sharding import PartitionSpec as P

NX, NY, NZ, NC = 4, 4, 8, 2
TB = 128
HB = TB // 2
QB = TB // 4
DF = 1024
FH = 1664
KC = HB * DF // 128
SCR = 16
REACH = 85.0
MESH = pl.DeviceIdType.MESH
F32, BF16 = jnp.float32, jnp.bfloat16


def rem(a, n):
    return lax.rem(a, n)


def kernel(
    act, og, w, ig_out, wg_out,
    G, AT, ABUF, W, WT, ACC, PT, PR, CS, CR, OUTB,
    ld, gs, gr, zs, zr, sas, sar, pss, psr, css, crs, outs,
):
    row, col = lax.axis_index("row"), lax.axis_index("col")
    z, k = row // NC, rem(row, NC)
    x, y = col // NY, rem(col, NY)

    def dev(dx, dy, dz, flip=False):
        kk = 1 - k if flip else k
        return (rem(z + dz + NZ, NZ) * NC + kk, rem(x + dx + NX, NX) * NY + rem(y + dy + NY, NY))

    def block_row(dx, dy):
        return (rem(x + dx + NX, NX) * NY + rem(y + dy + NY, NY)) * TB

    own = block_row(0, 0)
    load_g = pltpu.make_async_copy(og, G.at[pl.ds(pl.multiple_of(own, TB), TB)], ld.at[0])
    load_a = pltpu.make_async_copy(act, ABUF, ld.at[1])
    load_w = pltpu.make_async_copy(w, W, ld.at[2])
    load_a.start()
    load_g.start()
    load_w.start()

    partners = [dev(1, 0, 0), dev(-1, 0, 0), dev(0, 1, 0), dev(0, -1, 0), dev(0, 0, 1), dev(0, 0, -1), dev(0, 0, 0, True)]
    barrier = pltpu.get_barrier_semaphore()
    for d in partners:
        pl.semaphore_signal(barrier, inc=1, device_id=d, device_id_type=MESH)

    SIGN = (1, -1, 1, -1)

    def g_piece(di, j):
        s = SIGN[di]
        first, second = (0, HB) if di < 2 else (HB, 0)
        sub = 0 if s > 0 else QB
        along, perp, r0, n = (
            (0, 0, first, HB), (0, 0, second, HB), (-s, 0, first + sub, QB),
            (0, -1, second, HB), (0, 1, second, HB), (-s, 0, second + sub, QB),
            (0, 2, second, QB), (0, 2, second + QB, QB),
            (-s, -1, second + sub, QB), (-s, 1, second + sub, QB), (-s, 2, second + sub, QB),
        )[j]
        return along, perp, r0, n

    def g_copy(di, j, shift):
        along, perp, r0, n = g_piece(di, j)
        along = along - shift * SIGN[di]
        dx, dy = (along, perp) if di < 2 else (perp, along)
        ref = G.at[pl.ds(pl.multiple_of(block_row(dx, dy) + r0, QB), n)]
        s = SIGN[di]
        target = dev(s, 0, 0) if di < 2 else dev(0, s, 0)
        return pltpu.make_async_remote_copy(
            src_ref=ref, dst_ref=ref, send_sem=gs.at[di, j], recv_sem=gr.at[di, j],
            device_id=target, device_id_type=MESH)

    def g_send(di, j):
        g_copy(di, j, 0).start()

    def g_round(j):
        for di in range(4):
            s = SIGN[di]
            g_copy(di, j, 1).wait_recv()
            perp = (2, 3) if di < 2 else (0, 1)
            if j == 0:
                g_send(di, 2)
                for p in perp:
                    g_send(p, 3 if s > 0 else 4)
            elif j == 1:
                g_send(di, 5)
            elif j == 2:
                for p in perp:
                    g_send(p, 6 if s > 0 else 7)
            elif j == 3:
                g_send(di, 8)
            elif j == 4:
                g_send(di, 9)
            elif (j == 6 and s > 0) or (j == 7 and s < 0):
                g_send(di, 10)

    def a_ref(n, si, shift):
        s = 1 if si == 0 else -1
        d = (n // 2) if shift == 0 else (n // 2) + 1
        half = n % 2 if si == 0 else 1 - n % 2
        r = rem(z - s * d + NZ, NZ) * NC + k
        return AT.at[r, pl.ds(half * (DF // 2), DF // 2)]

    def a_copy(n, si, shift):
        ref = a_ref(n, si, shift)
        return pltpu.make_async_remote_copy(
            src_ref=ref, dst_ref=ref, send_sem=zs.at[si, n], recv_sem=zr.at[si, n],
            device_id=dev(0, 0, 1 if si == 0 else -1), device_id_type=MESH)

    SIB = (0, 1, -1, 2, -2, 3, -3, 4)

    def sib_copy(i, mine):
        r = rem(z - SIB[i] + NZ, NZ) * NC + (k if mine else 1 - k)
        return pltpu.make_async_remote_copy(
            src_ref=AT.at[r], dst_ref=AT.at[r], send_sem=sas.at[i], recv_sem=sar.at[i],
            device_id=dev(0, 0, 0, True), device_id_type=MESH)

    def a_round(n):
        for si in range(2):
            a_copy(n, si, 1).wait_recv()
            if n <= 4:
                a_copy(n + 2, si, 0).start()
            if n in (1, 3, 5):
                sib_copy(n + si, True).start()
        if n == 6:
            sib_copy(7, True).start()

    def ig_block(dxi, dyi):
        rows = pl.ds(pl.multiple_of(block_row(dxi, dyi), TB), TB)
        idx = dxi * NY + dyi
        for n0 in range(0, DF, 256):
            PT[idx, :, n0:n0 + 256] = jnp.dot(G[rows, :], WT[:, n0:n0 + 256], preferred_element_type=F32)

        @pl.when(rem(dyi + y + k, 2) == 1)
        def _():
            for h in range(2):
                p_copy(dxi, dyi, h).start()

    def p_copy(dxi, dyi, h):
        idx, slot = dxi * NY + dyi, dxi * 2 + dyi // 2
        half = pl.ds(h * HB, HB) if isinstance(h, int) else pl.ds(pl.multiple_of(h * HB, HB), HB)
        return pltpu.make_async_remote_copy(
            src_ref=PT.at[idx, half], dst_ref=PR.at[slot, half], send_sem=pss.at[idx, h], recv_sem=psr.at[slot, h],
            device_id=dev(0, 0, 0, True), device_id_type=MESH)

    def ig_batch(blocks):
        @pl.loop(0, len(blocks))
        def _(i):
            dxi = jnp.int32(blocks[-1][0])
            dyi = jnp.int32(blocks[-1][1])
            for q in range(len(blocks) - 1):
                dxi = jnp.where(i == q, blocks[q][0], dxi)
                dyi = jnp.where(i == q, blocks[q][1], dyi)
            ig_block(dxi, dyi)

    parity = rem(y + k, 2)

    def unit(u):
        m, h = u // 2, rem(u, 2)
        t = jnp.where(parity == 0, rem(m, 4), m // 2)
        dxi = jnp.where(t == 1, 3, jnp.where(t == 2, 1, jnp.where(t == 3, 2, 0)))
        dyi = jnp.where(parity == 0, 2 * (m // 4), 1 + 2 * rem(m, 2))
        bx, by = rem(x + dxi, NX), rem(y + dyi, NY)
        owner = 2 * bx + by // 2
        delta = rem(z - owner + NZ, NZ)
        eps = jnp.where(h == 0, delta, rem(NZ - delta, NZ))
        pos = jnp.where(eps == 0, 4, jnp.where(eps <= 3, 3 - eps, eps - 4))
        return dxi, dyi, h, eps, pos

    def c_copy(u, h, eps):
        step = jnp.where((eps >= 4) == (h == 0), 1, NZ - 1)
        slot = jnp.where(eps == 1, 1, 0)
        return pltpu.make_async_remote_copy(
            src_ref=CS.at[u], dst_ref=CR.at[u, slot], send_sem=css.at[u], recv_sem=crs.at[u, slot],
            device_id=(rem(z + step, NZ) * NC + k, col), device_id_type=MESH)

    def c_wait(u, slot):
        pltpu.make_async_remote_copy(
            src_ref=CS.at[u], dst_ref=CR.at[u, slot], send_sem=css.at[u], recv_sem=crs.at[u, slot],
            device_id=(row, col), device_id_type=MESH).wait_recv()

    def decode(u, slot, r, c, inv):
        code = CR[u, slot, pl.ds(pl.multiple_of(c * HB + r, 16), 16), :].astype(F32)
        mag = (jnp.log(jnp.abs(code)) + REACH) * inv
        return jnp.where(code < 0.0, -mag, mag)

    def reduce_unit(u, p):
        dxi, dyi, h, eps, pos = unit(u)
        idx, slot_p = dxi * NY + dyi, dxi * 2 + dyi // 2

        def total(r, c, invs):
            rr = pl.ds(pl.multiple_of(h * HB + r, 16), 16)
            cc = slice(c * 128, (c + 1) * 128)
            v = PT[idx, rr, cc] + PR[slot_p, rr, cc]
            for slot, inv in enumerate(invs):
                v = v + decode(u, slot, r, c, inv)
            return v

        def scales(n):
            return [CR[u, slot, KC:KC + SCR, :].astype(F32) * (1.0 / (2 * REACH)) for slot in range(n)]

        def relay(n):
            for slot in range(n):
                c_wait(u, slot)
            invs = scales(n)

            def body(i, top):
                r = i * 16
                rr = pl.ds(pl.multiple_of(h * HB + r, 16), 16)
                for c in range(8):
                    v = total(r, c, invs)
                    PT[idx, rr, c * 128:(c + 1) * 128] = v
                    top = jnp.maximum(top, jnp.abs(v))
                return top

            top = lax.fori_loop(0, HB // 16, body, jnp.zeros((16, 128), F32))
            scale = jnp.maximum(top * 1.01, 1e-30).astype(BF16)
            CS[u, KC:KC + SCR, :] = scale
            mul = (2 * REACH) / scale.astype(F32)

            @pl.loop(0, HB // 16)
            def _(i):
                r = i * 16
                rr = pl.ds(pl.multiple_of(h * HB + r, 16), 16)
                for c in range(8):
                    v = PT[idx, rr, c * 128:(c + 1) * 128]
                    code = jnp.exp(jnp.abs(v) * mul - REACH)
                    code = jnp.where(v < 0.0, -code, code)
                    CS[u, pl.ds(pl.multiple_of(c * HB + r, 16), 16), :] = code.astype(BF16)

            c_copy(u, h, eps).start()

        @pl.when(pos == p)
        def _():
            p_copy(dxi, dyi, h).wait_recv()
            if p == 0:
                relay(0)
            elif p < 4:
                relay(1)
            else:
                for slot in range(2):
                    c_wait(u, slot)
                invs = scales(2)

                @pl.loop(0, HB // 16)
                def _(i):
                    r = i * 16
                    rr = pl.ds(pl.multiple_of(h * HB + r, 16), 16)
                    for c in range(8):
                        OUTB[rr, c * 128:(c + 1) * 128] = total(r, c, invs).astype(BF16)

    def reduce_group(m0, m1, p):
        @pl.loop(2 * m0, 2 * m1)
        def _(u):
            reduce_unit(u, p)

    def wg_step(b0, nb, first, last):
        tm = 512
        rows = pl.ds(pl.multiple_of(b0 * TB, TB), nb * TB)

        @pl.loop(0, DF // tm)
        def _(mi):
            mm = pl.ds(pl.multiple_of(mi * tm, tm), tm)
            lhs = jnp.concatenate([AT[b0 + i, mm, :] for i in range(nb)], axis=1)
            for n0 in range(0, FH, 256):
                nn = slice(n0, min(n0 + 256, FH))
                v = jnp.dot(lhs, G[rows, nn], preferred_element_type=F32)
                if last:
                    W[mm, nn] = (ACC[mm, nn] + v).astype(BF16)
                elif first:
                    ACC[mm, nn] = v
                else:
                    ACC[mm, nn] = ACC[mm, nn] + v
            if last:
                pltpu.make_async_copy(W.at[mm], wg_out.at[mm], outs.at[mi]).start()

    def wt_chunk(j):
        WT[j * 128:(j + 1) * 128, :] = W[:, j * 128:(j + 1) * 128].T

    load_a.wait()
    for j in range(DF // 128):
        AT[row, j * 128:(j + 1) * 128, :] = ABUF[:, j * 128:(j + 1) * 128].T
    load_g.wait()
    pl.semaphore_wait(barrier, len(partners))
    for j in range(2):
        for di in range(4):
            g_send(di, j)
        for si in range(2):
            a_copy(j, si, 0).start()
    sib_copy(0, True).start()
    load_w.wait()
    for j in range(6):
        wt_chunk(j)
    a_round(0)
    for j in range(6, 10):
        wt_chunk(j)
    g_round(0)
    a_round(1)
    for j in range(10, FH // 128):
        wt_chunk(j)
    a_round(2)
    g_round(1)
    ig_batch([(0, 0), (1, 0), (3, 0)])
    a_round(3)
    g_round(2)
    ig_batch([(0, 1), (0, 3)])
    a_round(4)
    g_round(3)
    reduce_group(0, 2, 0)
    a_round(5)
    g_round(4)
    a_round(6)
    ig_batch([(3, 3), (3, 1), (1, 3), (1, 1)])
    g_round(5)
    reduce_group(0, 2, 1)
    ig_batch([(2, 0), (0, 2)])
    reduce_group(2, 5, 0)
    g_round(6)
    for i in range(8):
        sib_copy(i, False).wait_recv()
    bown = y // 2
    x1, x2, x3 = rem(x + 1, NX), rem(x + 2, NX), rem(x + 3, NX)
    wg_step(x * NY, 4, True, False)
    g_round(7)
    reduce_group(0, 2, 2)
    g_round(8)
    ig_batch([(3, 2), (2, 3)])
    reduce_group(2, 5, 1)
    reduce_group(0, 2, 3)
    g_round(9)
    ig_batch([(1, 2), (2, 1)])
    reduce_group(5, 7, 0)
    g_round(10)
    ig_batch([(2, 2)])
    reduce_group(7, 8, 0)
    reduce_group(2, 5, 2)
    reduce_group(0, 2, 4)
    wg_step(x1 * NY + 2 * bown, 2, False, False)
    reduce_group(5, 7, 1)
    reduce_group(7, 8, 1)
    reduce_group(2, 5, 3)
    wg_step(x3 * NY + 2 * bown, 2, False, False)
    reduce_group(5, 7, 2)
    reduce_group(7, 8, 2)
    reduce_group(2, 5, 4)
    wg_step(x1 * NY + 2 * (1 - bown), 2, False, False)
    reduce_group(5, 7, 3)
    reduce_group(7, 8, 3)
    wg_step(x3 * NY + 2 * (1 - bown), 2, False, False)
    wg_step(x2 * NY, 4, False, True)
    reduce_group(5, 8, 4)
    out_ig = pltpu.make_async_copy(OUTB, ig_out, ld.at[0])
    out_ig.start()

    for di in range(4):
        for j in range(11):
            g_copy(di, j, 0).wait_send()
    for si in range(2):
        for n in range(7):
            a_copy(n, si, 0).wait_send()
    for i in range(8):
        sib_copy(i, True).wait_send()

    @pl.loop(0, 16)
    def _(i):
        dxi, dyi = i // NY, rem(i, NY)

        @pl.when(rem(dyi + y + k, 2) == 1)
        def _():
            for h in range(2):
                p_copy(dxi, dyi, h).wait_send()

        _, _, h, eps, _ = unit(i)

        @pl.when(eps != 0)
        def _():
            c_copy(i, h, eps).wait_send()

    out_ig.wait()
    for mi in range(2):
        mm = pl.ds(mi * 512, 512)
        pltpu.make_async_copy(W.at[mm], wg_out.at[mm], outs.at[mi]).wait()


def per_device(activations, out_grad, weight):
    dma = pltpu.SemaphoreType.DMA
    vmem = pltpu.VMEM
    nblk = NX * NY
    anywhere = pl.BlockSpec(memory_space=pl.ANY)
    return pl.pallas_call(
        kernel,
        name="up_backward",
        out_shape=(jax.ShapeDtypeStruct((TB, DF), BF16), jax.ShapeDtypeStruct((DF, FH), BF16)),
        in_specs=[anywhere] * 3,
        out_specs=(anywhere, anywhere),
        scratch_shapes=[
            vmem((nblk * TB, FH), BF16),
            vmem((NZ * NC, DF, TB), BF16),
            vmem((TB, DF), BF16),
            vmem((DF, FH), BF16),
            vmem((FH, DF), BF16),
            vmem((DF, FH), F32),
            vmem((nblk, TB, DF), F32),
            vmem((nblk // 2, TB, DF), F32),
            vmem((nblk, KC + SCR, 128), BF16),
            vmem((nblk, 2, KC + SCR, 128), BF16),
            vmem((TB, DF), BF16),
            dma((3,)),
            dma((4, 11)), dma((4, 11)),
            dma((2, 7)), dma((2, 7)),
            dma((8,)), dma((8,)),
            dma((nblk, 2)), dma((nblk // 2, 2)),
            dma((nblk,)), dma((nblk, 2)),
            dma((2,)),
        ],
        cost_estimate=pl.CostEstimate(flops=4 * nblk * TB * DF * FH, bytes_accessed=8 * DF * FH, transcendentals=0),
        compiler_params=pltpu.CompilerParams(
            collective_id=0, has_side_effects=True, vmem_limit_bytes=60 << 20),
    )(activations, out_grad, weight)


def solution(mesh):
    placed = (P("row", "col"), P("col", "row"), P("col", "row"))
    return jax.shard_map(
        per_device,
        mesh=mesh,
        in_specs=placed,
        out_specs=(P("row", "col"), P("col", "row")),
        check_vma=False,
    )
```

time: 206 us -> 89.1 us (0.43)
  the two profiles are of different devices: /device:TPU:28 before, /device:TPU:5 now
where the time goes in v1:
time: 89.1 us; the launch traced here: 88.9 us
  Pallas kernels  82.7 us (93%)
  local copies, waits for them, and re-layouts  5.63 us (6%)
    pallas_call x1, Pallas kernels, per_device(): pl.pallas_call(kernel, name='up_backward', out_shape=(jax.ShapeDtypeStruc...  82.7 us
    unnamed x2, local copies, waits for them, and re-layouts  5.63 us

profile of v1, /device:TPU:5, one launch (start us, length us, event | category | flops | bytes accessed | tf_op | source)
XLA Modules:
  0.0 88.9 jit_solution(2930462700782580649)
XLA Ops:
  0.6 82.7 %up_backward.1 = (bf16[128,1024]{1,0:T(8,128)(2,1)}, bf16[1024,1664]{1,0:T(8,128)(2,1)}) custom-call(bf16[128,1024]{1,0:T(8,128)(2,1)} %act.1, bf16[128,1664]{1,0:T(8,128)(2,1)} %og.1, bf16[1024,1664]{1,0:T(8,128)(2,1)} %w.1), custom_call_target="tpu_custom_call" | custom-call | flops 13958643712 | bytes 13631488 | tf_op jit(solution)/shard_map/up_backward/pallas_call | solution.py:398
  83.3 1.7 %copy.7 = bf16[128,1024]{1,0:T(8,128)(2,1)} copy(bf16[128,1024]{1,0:T(8,128)(2,1)} %get-tuple-element.4) | data formatting | bytes 524288
  85.0 4.0 %copy.8 = bf16[1024,1664]{1,0:T(8,128)(2,1)} copy(bf16[1024,1664]{1,0:T(8,128)(2,1)} %get-tuple-element.5) | data formatting | bytes 6815744

commit v2 on v1

v2 whole, which is shorter than its diff:
```python
import functools

import jax
import jax.numpy as jnp
from jax import lax
from jax.experimental import pallas as pl
from jax.experimental.pallas import tpu as pltpu
from jax.sharding import PartitionSpec as P

NX, NY, NZ, NC = 4, 4, 8, 2
TB = 128
HB = TB // 2
QB = TB // 4
DF = 1024
FH = 1664
DH = DF // 2
KC = TB * DH // 128
SCR = 16
REACH = 85.0
MESH = pl.DeviceIdType.MESH
F32, BF16 = jnp.float32, jnp.bfloat16


TWO = ()
SCHEDULE = (
    ('t', 7), ('t', 6), ('i', ((0, 0),)), ('g', 0), ('a', 0), ('a', 1), ('a', 2), ('g', 1), ('i', ((0, 3), (3, 0))),
    ('a', 3), ('g', 2), ('r', (1,), 0), ('g', 3), ('g', 4), ('a', 4), ('i', ((3, 3), (1, 0), (3, 1))), ('g', 5),
    ('i', ((2, 0), (0, 2))), ('r', (2, 3), 0), ('i', ((0, 1), (1, 3), (1, 1))), ('r', (0,), 0), ('g', 6), ('g', 7),
    ('r', (4,), 0), ('a', 5), ('r', (3,), 1), ('a', 6), ('r', (1,), 1), ('g', 8), ('i', ((3, 2), (2, 3))),
    ('r', (5,), 0), ('g', 9), ('i', ((2, 1),)), ('r', (0, 2), 1), ('i', ((1, 2),)), ('r', (6,), 0), ('g', 10),
    ('i', ((2, 2),)), ('r', (7,), 0), ('s',), ('w', 'x'), ('r', (4, 5, 6), 1), ('r', (0,), 2), ('r', (7,), 1),
    ('w', '3p'), ('r', (1, 2, 3), 2), ('w', '1p'), ('r', (4, 5, 6, 7), 2), ('w', '2'),
    ('r', (0, 1, 2, 3, 4, 5, 6, 7), 3), ('w', '3o'), ('w', '1o'), ('r', (0, 1, 2, 3, 4, 5, 6, 7), 4),
)

def rem(a, n):
    return lax.rem(a, n)


def kernel(
    act, og, w, ig_out, wg_out,
    G, AT, ABUF, W, WT, ACC, PT, PR, CS, CR,
    ld, gs, gr, zs, zr, sas, sar, pss, psr, css, crs,
):
    row, col = lax.axis_index("row"), lax.axis_index("col")
    z, k = row // NC, rem(row, NC)
    x, y = col // NY, rem(col, NY)

    def dev(dx, dy, dz, flip=False):
        kk = 1 - k if flip else k
        return (rem(z + dz + NZ, NZ) * NC + kk, rem(x + dx + NX, NX) * NY + rem(y + dy + NY, NY))

    def block_row(dx, dy):
        return (rem(x + dx + NX, NX) * NY + rem(y + dy + NY, NY)) * TB

    own = block_row(0, 0)
    load_g = pltpu.make_async_copy(og, G.at[pl.ds(pl.multiple_of(own, TB), TB)], ld.at[0])
    load_a = pltpu.make_async_copy(act, ABUF, ld.at[1])
    load_w = pltpu.make_async_copy(w, W, ld.at[2])
    load_a.start()
    load_g.start()
    load_w.start()

    partners = [dev(1, 0, 0), dev(-1, 0, 0), dev(0, 1, 0), dev(0, -1, 0), dev(0, 0, 1), dev(0, 0, -1),
                dev(0, 0, 2), dev(0, 0, -2), dev(0, 0, 0, True)]
    barrier = pltpu.get_barrier_semaphore()
    for d in partners:
        pl.semaphore_signal(barrier, inc=1, device_id=d, device_id_type=MESH)

    SIGN = (1, -1, 1, -1)

    def g_piece(di, j):
        s = SIGN[di]
        first, second = (0, HB) if di < 2 else (HB, 0)
        sub = 0 if s > 0 else QB
        along, perp, r0, n = (
            (0, 0, first, HB), (0, 0, second, HB), (-s, 0, first + sub, QB),
            (0, -1, second, HB), (0, 1, second, HB), (-s, 0, second + sub, QB),
            (0, 2, second, QB), (0, 2, second + QB, QB),
            (-s, -1, second + sub, QB), (-s, 1, second + sub, QB), (-s, 2, second + sub, QB),
        )[j]
        return along, perp, r0, n

    def g_copy(di, j, shift):
        along, perp, r0, n = g_piece(di, j)
        along = along - shift * SIGN[di]
        dx, dy = (along, perp) if di < 2 else (perp, along)
        ref = G.at[pl.ds(pl.multiple_of(block_row(dx, dy) + r0, QB), n)]
        s = SIGN[di]
        target = dev(s, 0, 0) if di < 2 else dev(0, s, 0)
        return pltpu.make_async_remote_copy(
            src_ref=ref, dst_ref=ref, send_sem=gs.at[di, j], recv_sem=gr.at[di, j],
            device_id=target, device_id_type=MESH)

    def g_send(di, j):
        g_copy(di, j, 0).start()

    def g_round(j):
        for di in range(4):
            s = SIGN[di]
            g_copy(di, j, 1).wait_recv()
            perp = (2, 3) if di < 2 else (0, 1)
            if j == 0:
                g_send(di, 2)
                for p in perp:
                    g_send(p, 3 if s > 0 else 4)
            elif j == 1:
                g_send(di, 5)
            elif j == 2:
                for p in perp:
                    g_send(p, 6 if s > 0 else 7)
            elif j == 3:
                g_send(di, 8)
            elif j == 4:
                g_send(di, 9)
            elif (j == 6 and s > 0) or (j == 7 and s < 0):
                g_send(di, 10)

    def a_ref(n, si, shift):
        s = 1 if si == 0 else -1
        d = (n // 2) if shift == 0 else (n // 2) + 1
        half = n % 2 if si == 0 else 1 - n % 2
        r = rem(z - s * d + NZ, NZ) * NC + k
        return AT.at[r, pl.ds(half * (DF // 2), DF // 2)]

    def a_copy(n, si, shift):
        ref = a_ref(n, si, shift)
        return pltpu.make_async_remote_copy(
            src_ref=ref, dst_ref=ref, send_sem=zs.at[si, n], recv_sem=zr.at[si, n],
            device_id=dev(0, 0, 1 if si == 0 else -1), device_id_type=MESH)

    SIB = (0, 1, -1, 2, -2, 3, -3, 4)

    def sib_copy(i, mine):
        r = rem(z - SIB[i] + NZ, NZ) * NC + (k if mine else 1 - k)
        return pltpu.make_async_remote_copy(
            src_ref=AT.at[r], dst_ref=AT.at[r], send_sem=sas.at[i], recv_sem=sar.at[i],
            device_id=dev(0, 0, 0, True), device_id_type=MESH)

    def a_round(n):
        for si in range(2):
            a_copy(n, si, 1).wait_recv()
            if n <= 4:
                a_copy(n + 2, si, 0).start()
            if n in (1, 3, 5):
                sib_copy(n + si, True).start()
        if n == 6:
            sib_copy(7, True).start()

    def pick(i, values):
        v = jnp.int32(values[-1])
        for q, e in enumerate(values[:-1]):
            v = jnp.where(i == q, e, v)
        return v

    def ig_block(dxi, dyi):
        rows = pl.ds(pl.multiple_of(block_row(dxi, dyi), TB), TB)
        idx = dxi * NY + dyi

        @pl.loop(0, 2)
        def _(h):
            for n0 in range(0, DH, 256):
                cols = pl.ds(pl.multiple_of(h * DH + n0, 256), 256)
                PT[idx, h, :, n0:n0 + 256] = jnp.dot(G[rows, :], WT[:, cols], preferred_element_type=F32)

            @pl.when(rem(dyi + y + k, 2) == 1)
            def _():
                p_copy(dxi, dyi, h).start()

    def p_copy(dxi, dyi, h):
        idx, slot = dxi * NY + dyi, dxi * 2 + dyi // 2
        return pltpu.make_async_remote_copy(
            src_ref=PT.at[idx, h], dst_ref=PR.at[slot, h], send_sem=pss.at[idx, h], recv_sem=psr.at[slot, h],
            device_id=dev(0, 0, 0, True), device_id_type=MESH)

    def ig_batch(blocks):
        @pl.loop(0, len(blocks))
        def _(i):
            dxi, dyi = pick(i, [b[0] for b in blocks]), pick(i, [b[1] for b in blocks])
            ig_block(dxi, dyi)

    parity = rem(y + k, 2)

    def unit(u):
        m, h = u // 2, rem(u, 2)
        t = jnp.where(parity == 0, rem(m, 4), m // 2)
        dxi = jnp.where(t == 1, 3, jnp.where(t == 2, 1, jnp.where(t == 3, 2, 0)))
        dyi = jnp.where(parity == 0, 2 * (m // 4), 1 + 2 * rem(m, 2))
        bx, by = rem(x + dxi, NX), rem(y + dyi, NY)
        owner = 2 * bx + by // 2
        delta = rem(z - owner + NZ, NZ)
        eps = jnp.where(h == 0, delta, rem(NZ - delta, NZ))
        return dxi, dyi, h, eps

    def c_copy(u, h, eps, two):
        if two:
            dist = jnp.where((eps == 4) | (eps == 6) | (eps == 2), 2, 1)
            slot = jnp.where((eps == 4) | (eps == 1), 1, jnp.where(eps == 6, 2, jnp.where(eps == 2, 3, 0)))
        else:
            dist = 1
            slot = jnp.where(eps == 1, 1, 0)
        step = jnp.where((eps >= 4) == (h == 0), dist, NZ - dist)
        return pltpu.make_async_remote_copy(
            src_ref=CS.at[u], dst_ref=CR.at[u, slot], send_sem=css.at[u], recv_sem=crs.at[u, slot],
            device_id=(rem(z + step, NZ) * NC + k, col), device_id_type=MESH)

    def c_wait(u, slot):
        pltpu.make_async_remote_copy(
            src_ref=CS.at[u], dst_ref=CR.at[u, slot], send_sem=css.at[u], recv_sem=crs.at[u, slot],
            device_id=(row, col), device_id_type=MESH).wait_recv()

    def decode(u, slot, i, c, inv):
        code = CR[u, slot, pl.ds(pl.multiple_of(c * TB + i * 16, 16), 16), :].astype(F32)
        mag = (jnp.log(jnp.abs(code)) + REACH) * inv
        return jnp.where(code < 0.0, -mag, mag)

    def reduce_unit(u, p, two):
        dxi, dyi, h, eps = unit(u)
        idx, slot_p = dxi * NY + dyi, dxi * 2 + dyi // 2

        def collect(n):
            p_copy(dxi, dyi, h).wait_recv()
            for slot in range(n):
                c_wait(u, slot)
            return [CR[u, slot, KC:KC + SCR, :].astype(F32) * (1.0 / (2 * REACH)) for slot in range(n)]

        def total(i, c, invs):
            rr = pl.ds(pl.multiple_of(i * 16, 16), 16)
            cc = slice(c * 128, (c + 1) * 128)
            v = PT[idx, h, rr, cc] + PR[slot_p, h, rr, cc]
            for slot, inv in enumerate(invs):
                v = v + decode(u, slot, i, c, inv)
            return v

        def relay(n):
            invs = collect(n)

            def body(i, top):
                rr = pl.ds(pl.multiple_of(i * 16, 16), 16)
                for c in range(DH // 128):
                    v = total(i, c, invs)
                    PT[idx, h, rr, c * 128:(c + 1) * 128] = v
                    top = jnp.maximum(top, jnp.abs(v))
                return top

            top = lax.fori_loop(0, TB // 16, body, jnp.zeros((16, 128), F32))
            scale = jnp.maximum(top * 1.01, 1e-30).astype(BF16)
            CS[u, KC:KC + SCR, :] = scale
            mul = (2 * REACH) / scale.astype(F32)

            @pl.loop(0, TB // 16)
            def _(i):
                rr = pl.ds(pl.multiple_of(i * 16, 16), 16)
                for c in range(DH // 128):
                    v = PT[idx, h, rr, c * 128:(c + 1) * 128]
                    code = jnp.exp(jnp.abs(v) * mul - REACH)
                    code = jnp.where(v < 0.0, -code, code)
                    CS[u, pl.ds(pl.multiple_of(c * TB + i * 16, 16), 16), :] = code.astype(BF16)

            c_copy(u, h, eps, two).start()

        def finish(n):
            invs = collect(n)
            for half in range(2):
                @pl.when(h == half)
                def _():
                    @pl.loop(0, TB // 16)
                    def _(i):
                        rr = pl.ds(pl.multiple_of(i * 16, 16), 16)
                        for c in range(DH // 128):
                            c0 = half * DH + c * 128
                            ig_out[rr, c0:c0 + 128] = total(i, c, invs).astype(BF16)

        if two:
            if p == 0:
                pl.when((eps == 1) | (eps == 7) | ((eps >= 3) & (eps <= 5)))(lambda: relay(0))
            elif p == 1:
                pl.when(eps == 6)(lambda: relay(2))
                pl.when(eps == 2)(lambda: relay(1))
            else:
                pl.when(eps == 0)(lambda: finish(4))
        else:
            if p == 0:
                pl.when((eps == 4) | (eps == 3))(lambda: relay(0))
            elif p < 4:
                pl.when((eps == 4 + p) | ((eps == 3 - p) & (eps > 0)))(lambda: relay(1))
            else:
                pl.when(eps == 0)(lambda: finish(2))

    def reduce_group(ms, p):
        @pl.loop(0, 2 * len(ms))
        def _(i):
            reduce_unit(2 * pick(i // 2, ms) + rem(i, 2), p, ms[0] in TWO)

    def wg_step(b0, nb, first, last):
        tm = 512
        rows = pl.ds(pl.multiple_of(b0 * TB, TB), nb * TB)

        @pl.loop(0, DF // tm)
        def _(mi):
            mm = pl.ds(pl.multiple_of(mi * tm, tm), tm)
            lhs = jnp.concatenate([AT[b0 + i, mm, :] for i in range(nb)], axis=1)
            for n0 in range(0, FH, 256):
                nn = slice(n0, min(n0 + 256, FH))
                v = jnp.dot(lhs, G[rows, nn], preferred_element_type=F32)
                if last:
                    wg_out[mm, nn] = (ACC[mm, nn] + v).astype(BF16)
                elif first:
                    ACC[mm, nn] = v
                else:
                    ACC[mm, nn] = ACC[mm, nn] + v

    def wt_chunk(j):
        WT[j * 128:(j + 1) * 128, :] = W[:, j * 128:(j + 1) * 128].T

    load_a.wait()
    for j in range(DF // 128):
        AT[row, j * 128:(j + 1) * 128, :] = ABUF[:, j * 128:(j + 1) * 128].T
    load_g.wait()
    pl.semaphore_wait(barrier, len(partners))
    for j in range(2):
        for di in range(4):
            g_send(di, j)
        for si in range(2):
            a_copy(j, si, 0).start()
    sib_copy(0, True).start()
    load_w.wait()
    bown = y // 2
    x1, x2, x3 = rem(x + 1, NX), rem(x + 2, NX), rem(x + 3, NX)
    groups = {
        "x": (x * NY, 4), "2": (x2 * NY, 4),
        "1o": (x1 * NY + 2 * bown, 2), "1p": (x1 * NY + 2 * (1 - bown), 2),
        "3o": (x3 * NY + 2 * bown, 2), "3p": (x3 * NY + 2 * (1 - bown), 2),
    }
    wt_next, wg_done = 0, 0
    for what, *how in SCHEDULE:
        if what == "t":
            for j in range(wt_next, wt_next + how[0]):
                wt_chunk(j)
            wt_next += how[0]
        elif what == "g":
            g_round(how[0])
        elif what == "a":
            a_round(how[0])
        elif what == "i":
            ig_batch(how[0])
        elif what == "s":
            for i in range(8):
                sib_copy(i, False).wait_recv()
        elif what == "w":
            wg_step(*groups[how[0]], wg_done == 0, wg_done == 5)
            wg_done += 1
        else:
            reduce_group(*how)

    for di in range(4):
        for j in range(11):
            g_copy(di, j, 0).wait_send()
    for si in range(2):
        for n in range(7):
            a_copy(n, si, 0).wait_send()
    for i in range(8):
        sib_copy(i, True).wait_send()

    @pl.loop(0, 16)
    def _(i):
        dxi, dyi = i // NY, rem(i, NY)

        @pl.when(rem(dyi + y + k, 2) == 1)
        def _():
            for h in range(2):
                p_copy(dxi, dyi, h).wait_send()

        _, _, h, eps = unit(i)

        @pl.when(eps != 0)
        def _():
            c_copy(i, h, eps, False).wait_send()


def hand_out(ig, wg, ig_out, wg_out, sems):
    n = sems.shape[0] - 1
    rows = DF // n
    copies = [pltpu.make_async_copy(wg.at[pl.ds(i * rows, rows)], wg_out.at[pl.ds(i * rows, rows)], sems.at[i])
              for i in range(n)]
    copies.append(pltpu.make_async_copy(ig, ig_out, sems.at[n]))
    for c in copies:
        c.start()
    for c in copies:
        c.wait()


def per_device(activations, out_grad, weight):
    dma = pltpu.SemaphoreType.DMA
    vmem = pltpu.VMEM
    nblk = NX * NY
    anywhere = pl.BlockSpec(memory_space=pl.ANY)
    sums = pl.pallas_call(
        kernel,
        name="up_backward",
        out_shape=(vmem((TB, DF), BF16), vmem((DF, FH), BF16)),
        in_specs=[anywhere] * 3,
        out_specs=(pl.BlockSpec(memory_space=vmem),) * 2,
        scratch_shapes=[
            vmem((nblk * TB, FH), BF16),
            vmem((NZ * NC, DF, TB), BF16),
            vmem((TB, DF), BF16),
            vmem((DF, FH), BF16),
            vmem((FH, DF), BF16),
            vmem((DF, FH), F32),
            vmem((nblk, 2, TB, DH), F32),
            vmem((nblk // 2, 2, TB, DH), F32),
            vmem((nblk, KC + SCR, 128), BF16),
            vmem((nblk, 4, KC + SCR, 128), BF16),
            dma((3,)),
            dma((4, 11)), dma((4, 11)),
            dma((2, 7)), dma((2, 7)),
            dma((8,)), dma((8,)),
            dma((nblk, 2)), dma((nblk // 2, 2)),
            dma((nblk,)), dma((nblk, 4)),
        ],
        cost_estimate=pl.CostEstimate(flops=4 * nblk * TB * DF * FH, bytes_accessed=8 * DF * FH, transcendentals=0),
        compiler_params=pltpu.CompilerParams(
            collective_id=0, has_side_effects=True, vmem_limit_bytes=52 << 20),
    )(activations, out_grad, weight)
    return pl.pallas_call(
        hand_out,
        name="hand_out",
        out_shape=(jax.ShapeDtypeStruct((TB, DF), BF16), jax.ShapeDtypeStruct((DF, FH), BF16)),
        in_specs=[pl.BlockSpec(memory_space=vmem)] * 2,
        out_specs=(anywhere, anywhere),
        scratch_shapes=[dma((17,))],
    )(*sums)


def solution(mesh):
    placed = (P("row", "col"), P("col", "row"), P("col", "row"))
    return jax.shard_map(
        per_device,
        mesh=mesh,
        in_specs=placed,
        out_specs=(P("row", "col"), P("col", "row")),
        check_vma=False,
    )
```

time: 89.1 us -> 80 us (0.90)
  the two profiles are of different devices: /device:TPU:5 before, /device:TPU:28 now
where the time goes in v2:
time: 80 us; the launch traced here: 79.9 us
  Pallas kernels  76.8 us (96%)
  local copies, waits for them, and re-layouts  2.43 us (3%)
    pallas_call x1, Pallas kernels, per_device(): pl.pallas_call(kernel, name='up_backward', out_shape=(vmem((TB, DF), BF16...  72.8 us
    pallas_call x1, Pallas kernels, per_device(): pl.pallas_call(hand_out, name='hand_out', out_shape=(jax.ShapeDtypeStruct...  4.03 us
    unnamed x4, local copies, waits for them, and re-layouts  2.43 us

profile of v2, /device:TPU:28, one launch (start us, length us, event | category | flops | bytes accessed | tf_op | source)
XLA Modules:
  0.0 79.9 jit_solution(11638401741142132045)
XLA Ops:
  0.6 72.8 %up_backward.1 = (bf16[128,1024]{1,0:T(8,128)(2,1)S(1)}, bf16[1024,1664]{1,0:T(8,128)(2,1)S(1)}) custom-call(bf16[128,1024]{1,0:T(8,128)(2,1)} %act.1, bf16[128,1664]{1,0:T(8,128)(2,1)} %og.1, bf16[1024,1664]{1,0:T(8,128)(2,1)} %w.1), custom_call_target="tpu_custom_call" | custom-call | flops 13958643712 | bytes 13631488 | tf_op jit(solution)/shard_map/up_backward/pallas_call | solution.py:398
  73.4 0.0 copy-start
  73.4 1.7 %copy-done = bf16[1024,1664]{1,0:T(8,128)(2,1)} copy-done((bf16[1024,1664]{1,0:T(8,128)(2,1)}, bf16[1024,1664]{1,0:T(8,128)(2,1)S(1)}, u32[]{:S(2)}) %copy-start) | copy-done | bytes 3407896
  75.1 0.0 copy-start.1
  75.1 0.7 copy-done.1
  75.8 4.0 %hand_out.1 = (bf16[128,1024]{1,0:T(8,128)(2,1)}, bf16[1024,1664]{1,0:T(8,128)(2,1)}) custom-call(bf16[128,1024]{1,0:T(8,128)(2,1)} %copy-done.1, bf16[1024,1664]{1,0:T(8,128)(2,1)} %copy-done), custom_call_target="tpu_custom_call" | custom-call | tf_op jit(solution)/shard_map/hand_out/pallas_call | solution.py:426
Async XLA Ops:
  73.4 1.7 %copy-start = (bf16[1024,1664]{1,0:T(8,128)(2,1)}, bf16[1024,1664]{1,0:T(8,128)(2,1)S(1)}, u32[]{:S(2)}) copy-start(bf16[1024,1664]{1,0:T(8,128)(2,1)S(1)} %get-tuple-element.5.wg) | copy-start | bytes 10223620
  75.1 0.7 copy-start.1

commit v3 on v2

--- a/solution.py
+++ b/solution.py
@@ -23,14 +23,16 @@
 
 TWO = ()
 SCHEDULE = (
-    ('t', 7), ('t', 6), ('i', ((0, 0),)), ('g', 0), ('a', 0), ('a', 1), ('a', 2), ('g', 1), ('i', ((0, 3), (3, 0))),
-    ('a', 3), ('g', 2), ('r', (1,), 0), ('g', 3), ('g', 4), ('a', 4), ('i', ((3, 3), (1, 0), (3, 1))), ('g', 5),
-    ('i', ((2, 0), (0, 2))), ('r', (2, 3), 0), ('i', ((0, 1), (1, 3), (1, 1))), ('r', (0,), 0), ('g', 6), ('g', 7),
-    ('r', (4,), 0), ('a', 5), ('r', (3,), 1), ('a', 6), ('r', (1,), 1), ('g', 8), ('i', ((3, 2), (2, 3))),
-    ('r', (5,), 0), ('g', 9), ('i', ((2, 1),)), ('r', (0, 2), 1), ('i', ((1, 2),)), ('r', (6,), 0), ('g', 10),
-    ('i', ((2, 2),)), ('r', (7,), 0), ('s',), ('w', 'x'), ('r', (4, 5, 6), 1), ('r', (0,), 2), ('r', (7,), 1),
-    ('w', '3p'), ('r', (1, 2, 3), 2), ('w', '1p'), ('r', (4, 5, 6, 7), 2), ('w', '2'),
-    ('r', (0, 1, 2, 3, 4, 5, 6, 7), 3), ('w', '3o'), ('w', '1o'), ('r', (0, 1, 2, 3, 4, 5, 6, 7), 4),
+    ('t', 7), ('t', 6), ('i', ((0, 0),)), ('a', 0), ('g', 0), ('g', 1), ('i', ((0, 1), (0, 3))), ('a', 1),
+    ('i', ((1, 0), (3, 0))), ('a', 2), ('a', 3), ('g', 2), ('r', (0,), 0), ('g', 3), ('g', 4),
+    ('i', ((3, 3), (3, 1))), ('a', 4), ('i', ((1, 3), (1, 1))), ('g', 5), ('r', (2,), 0), ('i', ((2, 0), (0, 2))),
+    ('r', (3, 4), 0), ('g', 6), ('g', 7), ('r', (1,), 0), ('r', (3,), 1), ('a', 5), ('g', 8), ('i', ((3, 2), (2, 3))),
+    ('r', (5,), 0), ('a', 6), ('r', (2,), 1), ('g', 9), ('i', ((1, 2), (2, 1))), ('r', (3,), 2), ('r', (4,), 1),
+    ('r', (6,), 0), ('r', (0,), 1), ('s',), ('g', 10), ('i', ((2, 2),)), ('r', (7,), 0), ('w', '1', 1),
+    ('r', (5,), 1), ('w', '0', 1), ('r', (1, 6), 1), ('w', '2', 0), ('r', (2,), 2), ('r', (7,), 1), ('r', (0,), 2),
+    ('w', '0', 0), ('r', (1, 4, 5), 2), ('w', '3', 0), ('r', (6,), 2), ('w', '3', 1), ('r', (7,), 2),
+    ('r', (0, 1, 4, 5), 3), ('w', '1', 0), ('r', (2, 3), 3), ('w', '2', 1), ('r', (7,), 3), ('r', (4,), 4),
+    ('r', (6,), 3), ('r', (0, 1, 2, 3, 5, 6, 7), 4),
 )
 
 def rem(a, n):
@@ -153,31 +155,25 @@
             v = jnp.where(i == q, e, v)
         return v
 
-    def ig_block(dxi, dyi):
-        rows = pl.ds(pl.multiple_of(block_row(dxi, dyi), TB), TB)
-        idx = dxi * NY + dyi
-
-        @pl.loop(0, 2)
-        def _(h):
+    def ig_blocks(blocks):
+        rows = [pl.ds(pl.multiple_of(block_row(dxi, dyi), TB), TB) for dxi, dyi in blocks]
+
+        for h in range(2):
             for n0 in range(0, DH, 256):
-                cols = pl.ds(pl.multiple_of(h * DH + n0, 256), 256)
-                PT[idx, h, :, n0:n0 + 256] = jnp.dot(G[rows, :], WT[:, cols], preferred_element_type=F32)
-
-            @pl.when(rem(dyi + y + k, 2) == 1)
-            def _():
-                p_copy(dxi, dyi, h).start()
+                lhs = jnp.concatenate([G[r, :] for r in rows], axis=0)
+                d = jnp.dot(lhs, WT[:, h * DH + n0:h * DH + n0 + 256], preferred_element_type=F32)
+                for i, (dxi, dyi) in enumerate(blocks):
+                    PT[dxi * NY + dyi, h, :, n0:n0 + 256] = d[i * TB:(i + 1) * TB]
+            for dxi, dyi in blocks:
+                @pl.when(rem(dyi + y + k, 2) == 1)
+                def _():
+                    p_copy(dxi, dyi, h).start()
 
     def p_copy(dxi, dyi, h):
         idx, slot = dxi * NY + dyi, dxi * 2 + dyi // 2
         return pltpu.make_async_remote_copy(
             src_ref=PT.at[idx, h], dst_ref=PR.at[slot, h], send_sem=pss.at[idx, h], recv_sem=psr.at[slot, h],
             device_id=dev(0, 0, 0, True), device_id_type=MESH)
-
-    def ig_batch(blocks):
-        @pl.loop(0, len(blocks))
-        def _(i):
-            dxi, dyi = pick(i, [b[0] for b in blocks]), pick(i, [b[1] for b in blocks])
-            ig_block(dxi, dyi)
 
     parity = rem(y + k, 2)
 
@@ -243,12 +239,12 @@
                     top = jnp.maximum(top, jnp.abs(v))
                 return top
 
-            top = lax.fori_loop(0, TB // 16, body, jnp.zeros((16, 128), F32))
+            top = lax.fori_loop(0, TB // 16, body, jnp.zeros((16, 128), F32), unroll=TB // 16)
             scale = jnp.maximum(top * 1.01, 1e-30).astype(BF16)
             CS[u, KC:KC + SCR, :] = scale
             mul = (2 * REACH) / scale.astype(F32)
 
-            @pl.loop(0, TB // 16)
+            @pl.loop(0, TB // 16, unroll=TB // 16)
             def _(i):
                 rr = pl.ds(pl.multiple_of(i * 16, 16), 16)
                 for c in range(DH // 128):
@@ -264,7 +260,7 @@
             for half in range(2):
                 @pl.when(h == half)
                 def _():
-                    @pl.loop(0, TB // 16)
+                    @pl.loop(0, TB // 16, unroll=TB // 16)
                     def _(i):
                         rr = pl.ds(pl.multiple_of(i * 16, 16), 16)
                         for c in range(DH // 128):
@@ -292,23 +288,18 @@
         def _(i):
             reduce_unit(2 * pick(i // 2, ms) + rem(i, 2), p, ms[0] in TWO)
 
-    def wg_step(b0, nb, first, last):
-        tm = 512
-        rows = pl.ds(pl.multiple_of(b0 * TB, TB), nb * TB)
-
-        @pl.loop(0, DF // tm)
-        def _(mi):
-            mm = pl.ds(pl.multiple_of(mi * tm, tm), tm)
-            lhs = jnp.concatenate([AT[b0 + i, mm, :] for i in range(nb)], axis=1)
-            for n0 in range(0, FH, 256):
-                nn = slice(n0, min(n0 + 256, FH))
-                v = jnp.dot(lhs, G[rows, nn], preferred_element_type=F32)
-                if last:
-                    wg_out[mm, nn] = (ACC[mm, nn] + v).astype(BF16)
-                elif first:
-                    ACC[mm, nn] = v
-                else:
-                    ACC[mm, nn] = ACC[mm, nn] + v
+    def wg_step(b0, n0, n1, first, last):
+        rows = pl.ds(pl.multiple_of(b0 * TB, TB), NY * TB)
+        lhs = jnp.concatenate([AT[b0 + i] for i in range(NY)], axis=1)
+        for n in range(n0, n1, 256):
+            nn = slice(n, min(n + 256, n1))
+            v = jnp.dot(lhs, G[rows, nn], preferred_element_type=F32)
+            if last:
+                wg_out[:, nn] = (ACC[:, nn] + v).astype(BF16)
+            elif first:
+                ACC[:, nn] = v
+            else:
+                ACC[:, nn] = ACC[:, nn] + v
 
     def wt_chunk(j):
         WT[j * 128:(j + 1) * 128, :] = W[:, j * 128:(j + 1) * 128].T
@@ -325,14 +316,9 @@
             a_copy(j, si, 0).start()
     sib_copy(0, True).start()
     load_w.wait()
-    bown = y // 2
-    x1, x2, x3 = rem(x + 1, NX), rem(x + 2, NX), rem(x + 3, NX)
-    groups = {
-        "x": (x * NY, 4), "2": (x2 * NY, 4),
-        "1o": (x1 * NY + 2 * bown, 2), "1p": (x1 * NY + 2 * (1 - bown), 2),
-        "3o": (x3 * NY + 2 * bown, 2), "3p": (x3 * NY + 2 * (1 - bown), 2),
-    }
-    wt_next, wg_done = 0, 0
+    groups = {name: rem(x + int(name), NX) * NY for name in "0123"}
+    wt_next, wg_done = 0, [0, 0]
+    columns = ((0, 1024), (1024, FH))
     for what, *how in SCHEDULE:
         if what == "t":
             for j in range(wt_next, wt_next + how[0]):
@@ -343,13 +329,14 @@
         elif what == "a":
             a_round(how[0])
         elif what == "i":
-            ig_batch(how[0])
+            ig_blocks(how[0])
         elif what == "s":
             for i in range(8):
                 sib_copy(i, False).wait_recv()
         elif what == "w":
-            wg_step(*groups[how[0]], wg_done == 0, wg_done == 5)
-            wg_done += 1
+            part = how[1]
+            wg_step(groups[how[0]], *columns[part], wg_done[part] == 0, wg_done[part] == 3)
+            wg_done[part] += 1
         else:
             reduce_group(*how)
 
@@ -430,6 +417,7 @@
         in_specs=[pl.BlockSpec(memory_space=vmem)] * 2,
         out_specs=(anywhere, anywhere),
         scratch_shapes=[dma((17,))],
+        compiler_params=pltpu.CompilerParams(vmem_limit_bytes=1 << 20),
     )(*sums)
 
 

time: 80 us -> 75.9 us (0.949); the launches traced: 79.9 us -> 74.8 us
  Pallas kernels: 76.8 us -> 74 us
  local copies, waits for them, and re-layouts: 2.43 us -> 0 us
    unnamed x4 -> x0, local copies, waits for them, and re-layouts: 2.43 us -> none
    pallas_call x1, Pallas kernels: 4.03 us -> 1.98 us  [per_device(): pl.pallas_call(hand_out, name='hand_out', out_shape=(jax.ShapeDtypeStruct...]
where the time goes in v3:
time: 75.9 us; the launch traced here: 74.8 us
  Pallas kernels  74 us (97%)
  between operations  0.82 us (1%)
    pallas_call x1, Pallas kernels, per_device(): pl.pallas_call(kernel, name='up_backward', out_shape=(vmem((TB, DF), BF16...  72 us
    pallas_call x1, Pallas kernels, per_device(): pl.pallas_call(hand_out, name='hand_out', out_shape=(jax.ShapeDtypeStruct...  1.98 us

profile of v3, /device:TPU:28, one launch (start us, length us, event | category | flops | bytes accessed | tf_op | source)
XLA Modules:
  0.0 74.8 jit_solution(3561328869089772156)
XLA Ops:
  0.6 72.0 %up_backward.1 = (bf16[128,1024]{1,0:T(8,128)(2,1)S(1)}, bf16[1024,1664]{1,0:T(8,128)(2,1)S(1)}) custom-call(bf16[128,1024]{1,0:T(8,128)(2,1)} %act.1, bf16[128,1664]{1,0:T(8,128)(2,1)} %og.1, bf16[1024,1664]{1,0:T(8,128)(2,1)} %w.1), custom_call_target="tpu_custom_call" | custom-call | flops 13958643712 | bytes 13631488 | tf_op jit(solution)/shard_map/up_backward/pallas_call | solution.py:385
  72.7 2.0 %hand_out.1 = (bf16[128,1024]{1,0:T(8,128)(2,1)}, bf16[1024,1664]{1,0:T(8,128)(2,1)}) custom-call(bf16[128,1024]{1,0:T(8,128)(2,1)S(1)} %get-tuple-element.4.ig, bf16[1024,1664]{1,0:T(8,128)(2,1)S(1)} %get-tuple-element.5.wg), custom_call_target="tpu_custom_call" | custom-call | tf_op jit(solution)/shard_map/hand_out/pallas_call | solution.py:413

commit v4 on v3

--- a/solution.py
+++ b/solution.py
@@ -21,18 +21,18 @@
 F32, BF16 = jnp.float32, jnp.bfloat16
 
 
-TWO = ()
 SCHEDULE = (
-    ('t', 7), ('t', 6), ('i', ((0, 0),)), ('a', 0), ('g', 0), ('g', 1), ('i', ((0, 1), (0, 3))), ('a', 1),
-    ('i', ((1, 0), (3, 0))), ('a', 2), ('a', 3), ('g', 2), ('r', (0,), 0), ('g', 3), ('g', 4),
-    ('i', ((3, 3), (3, 1))), ('a', 4), ('i', ((1, 3), (1, 1))), ('g', 5), ('r', (2,), 0), ('i', ((2, 0), (0, 2))),
-    ('r', (3, 4), 0), ('g', 6), ('g', 7), ('r', (1,), 0), ('r', (3,), 1), ('a', 5), ('g', 8), ('i', ((3, 2), (2, 3))),
-    ('r', (5,), 0), ('a', 6), ('r', (2,), 1), ('g', 9), ('i', ((1, 2), (2, 1))), ('r', (3,), 2), ('r', (4,), 1),
-    ('r', (6,), 0), ('r', (0,), 1), ('s',), ('g', 10), ('i', ((2, 2),)), ('r', (7,), 0), ('w', '1', 1),
-    ('r', (5,), 1), ('w', '0', 1), ('r', (1, 6), 1), ('w', '2', 0), ('r', (2,), 2), ('r', (7,), 1), ('r', (0,), 2),
-    ('w', '0', 0), ('r', (1, 4, 5), 2), ('w', '3', 0), ('r', (6,), 2), ('w', '3', 1), ('r', (7,), 2),
-    ('r', (0, 1, 4, 5), 3), ('w', '1', 0), ('r', (2, 3), 3), ('w', '2', 1), ('r', (7,), 3), ('r', (4,), 4),
-    ('r', (6,), 3), ('r', (0, 1, 2, 3, 5, 6, 7), 4),
+    ('t', 7), ('t', 6), ('g', 0), ('a', 0), ('a', 1), ('a', 2), ('g', 1), ('i', ((0, 1), (0, 3))), ('g', 2), ('a', 3),
+    ('i', ((1, 0), (3, 0))), ('r', 'first', (1,)), ('i', ((0, 0),)), ('g', 3), ('g', 4), ('r', 'first', (0,)),
+    ('i', ((3, 3), (3, 1))), ('a', 4), ('i', ((1, 3), (1, 1))), ('r', 'middle', ((1, 1),)), ('g', 5),
+    ('i', ((2, 0), (0, 2))), ('r', 'first', (3,)), ('g', 6), ('r', 'first', (2,)), ('g', 7), ('r', 'first', (4,)),
+    ('a', 5), ('a', 6), ('g', 8), ('i', ((3, 2), (2, 3))), ('r', 'middle', ((3, 1), (1, 2))), ('r', 'first', (5,)),
+    ('r', 'middle', ((2, 1),)), ('g', 9), ('i', ((1, 2), (2, 1))), ('g', 10), ('r', 'first', (6,)), ('i', ((2, 2),)),
+    ('r', 'first', (7,)), ('r', 'middle', ((0, 1),)), ('s',), ('w', '1', 0), ('r', 'middle', ((4, 1), (5, 1))),
+    ('w', '2', 1), ('r', 'middle', ((2, 2), (6, 1), (7, 1))), ('w', '0', 0), ('r', 'middle', ((3, 2), (0, 2))),
+    ('w', '1', 1), ('r', 'middle', ((5, 2), (4, 2))), ('w', '2', 0), ('r', 'middle', ((6, 2), (7, 2))), ('w', '3', 1),
+    ('w', '3', 0), ('r', 'middle', ((4, 3), (0, 3), (2, 3), (5, 3), (3, 3), (6, 3), (7, 3), (1, 3))), ('w', '0', 1),
+    ('r', 'last', (2, 1, 5, 3, 4, 0, 6, 7)),
 )
 
 def rem(a, n):
@@ -64,7 +64,7 @@
     load_w.start()
 
     partners = [dev(1, 0, 0), dev(-1, 0, 0), dev(0, 1, 0), dev(0, -1, 0), dev(0, 0, 1), dev(0, 0, -1),
-                dev(0, 0, 2), dev(0, 0, -2), dev(0, 0, 0, True)]
+                dev(0, 0, 0, True)]
     barrier = pltpu.get_barrier_semaphore()
     for d in partners:
         pl.semaphore_signal(barrier, inc=1, device_id=d, device_id_type=MESH)
@@ -188,14 +188,9 @@
         eps = jnp.where(h == 0, delta, rem(NZ - delta, NZ))
         return dxi, dyi, h, eps
 
-    def c_copy(u, h, eps, two):
-        if two:
-            dist = jnp.where((eps == 4) | (eps == 6) | (eps == 2), 2, 1)
-            slot = jnp.where((eps == 4) | (eps == 1), 1, jnp.where(eps == 6, 2, jnp.where(eps == 2, 3, 0)))
-        else:
-            dist = 1
-            slot = jnp.where(eps == 1, 1, 0)
-        step = jnp.where((eps >= 4) == (h == 0), dist, NZ - dist)
+    def c_copy(u, h, eps):
+        slot = jnp.where(eps == 1, 1, 0)
+        step = jnp.where((eps >= 4) == (h == 0), 1, NZ - 1)
         return pltpu.make_async_remote_copy(
             src_ref=CS.at[u], dst_ref=CR.at[u, slot], send_sem=css.at[u], recv_sem=crs.at[u, slot],
             device_id=(rem(z + step, NZ) * NC + k, col), device_id_type=MESH)
@@ -210,7 +205,7 @@
         mag = (jnp.log(jnp.abs(code)) + REACH) * inv
         return jnp.where(code < 0.0, -mag, mag)
 
-    def reduce_unit(u, p, two):
+    def reduce_unit(u, p):
         dxi, dyi, h, eps = unit(u)
         idx, slot_p = dxi * NY + dyi, dxi * 2 + dyi // 2
 
@@ -239,12 +234,12 @@
                     top = jnp.maximum(top, jnp.abs(v))
                 return top
 
-            top = lax.fori_loop(0, TB // 16, body, jnp.zeros((16, 128), F32), unroll=TB // 16)
+            top = lax.fori_loop(0, TB // 16, body, jnp.zeros((16, 128), F32))
             scale = jnp.maximum(top * 1.01, 1e-30).astype(BF16)
             CS[u, KC:KC + SCR, :] = scale
             mul = (2 * REACH) / scale.astype(F32)
 
-            @pl.loop(0, TB // 16, unroll=TB // 16)
+            @pl.loop(0, TB // 16)
             def _(i):
                 rr = pl.ds(pl.multiple_of(i * 16, 16), 16)
                 for c in range(DH // 128):
@@ -253,40 +248,35 @@
                     code = jnp.where(v < 0.0, -code, code)
                     CS[u, pl.ds(pl.multiple_of(c * TB + i * 16, 16), 16), :] = code.astype(BF16)
 
-            c_copy(u, h, eps, two).start()
+            c_copy(u, h, eps).start()
 
         def finish(n):
             invs = collect(n)
             for half in range(2):
                 @pl.when(h == half)
                 def _():
-                    @pl.loop(0, TB // 16, unroll=TB // 16)
+                    @pl.loop(0, TB // 16)
                     def _(i):
                         rr = pl.ds(pl.multiple_of(i * 16, 16), 16)
                         for c in range(DH // 128):
                             c0 = half * DH + c * 128
                             ig_out[rr, c0:c0 + 128] = total(i, c, invs).astype(BF16)
 
-        if two:
-            if p == 0:
-                pl.when((eps == 1) | (eps == 7) | ((eps >= 3) & (eps <= 5)))(lambda: relay(0))
-            elif p == 1:
-                pl.when(eps == 6)(lambda: relay(2))
-                pl.when(eps == 2)(lambda: relay(1))
+        if p is None:
+            pl.when(eps == 0)(lambda: finish(2))
+        elif isinstance(p, int):
+            pl.when((eps == 4) | (eps == 3))(lambda: relay(0))
+        else:
+            pl.when((eps == 4 + p) | ((eps == 3 - p) & (eps > 0)))(lambda: relay(1))
+
+    def reduce_group(kind, items):
+        @pl.loop(0, 2 * len(items))
+        def _(i):
+            j, h = i // 2, rem(i, 2)
+            if kind == "middle":
+                reduce_unit(2 * pick(j, [m for m, _ in items]) + h, pick(j, [p for _, p in items]))
             else:
-                pl.when(eps == 0)(lambda: finish(4))
-        else:
-            if p == 0:
-                pl.when((eps == 4) | (eps == 3))(lambda: relay(0))
-            elif p < 4:
-                pl.when((eps == 4 + p) | ((eps == 3 - p) & (eps > 0)))(lambda: relay(1))
-            else:
-                pl.when(eps == 0)(lambda: finish(2))
-
-    def reduce_group(ms, p):
-        @pl.loop(0, 2 * len(ms))
-        def _(i):
-            reduce_unit(2 * pick(i // 2, ms) + rem(i, 2), p, ms[0] in TWO)
+                reduce_unit(2 * pick(j, items) + h, 0 if kind == "first" else None)
 
     def wg_step(b0, n0, n1, first, last):
         rows = pl.ds(pl.multiple_of(b0 * TB, TB), NY * TB)
@@ -362,7 +352,7 @@
 
         @pl.when(eps != 0)
         def _():
-            c_copy(i, h, eps, False).wait_send()
+            c_copy(i, h, eps).wait_send()
 
 
 def hand_out(ig, wg, ig_out, wg_out, sems):
@@ -398,13 +388,13 @@
             vmem((nblk, 2, TB, DH), F32),
             vmem((nblk // 2, 2, TB, DH), F32),
             vmem((nblk, KC + SCR, 128), BF16),
-            vmem((nblk, 4, KC + SCR, 128), BF16),
+            vmem((nblk, 2, KC + SCR, 128), BF16),
             dma((3,)),
             dma((4, 11)), dma((4, 11)),
             dma((2, 7)), dma((2, 7)),
             dma((8,)), dma((8,)),
             dma((nblk, 2)), dma((nblk // 2, 2)),
-            dma((nblk,)), dma((nblk, 4)),
+            dma((nblk,)), dma((nblk, 2)),
         ],
         cost_estimate=pl.CostEstimate(flops=4 * nblk * TB * DF * FH, bytes_accessed=8 * DF * FH, transcendentals=0),
         compiler_params=pltpu.CompilerParams(

time: 75.9 us -> 78.2 us (1.030)
  Pallas kernels: 74 us -> 76.3 us
    pallas_call x1, Pallas kernels: 72 us -> 74.3 us  [per_device(): pl.pallas_call(kernel, name='up_backward', out_shape=(vmem((TB, DF), BF16...]
where the time goes in v4:
time: 78.2 us; the launch traced here: 77.1 us
  Pallas kernels  76.3 us (98%)
  between operations  0.82 us (1%)
    pallas_call x1, Pallas kernels, per_device(): pl.pallas_call(kernel, name='up_backward', out_shape=(vmem((TB, DF), BF16...  74.3 us
    pallas_call x1, Pallas kernels, per_device(): pl.pallas_call(hand_out, name='hand_out', out_shape=(jax.ShapeDtypeStruct...  1.98 us

profile of v4, /device:TPU:28, one launch (start us, length us, event | category | flops | bytes accessed | tf_op | source)
XLA Modules:
  0.0 77.1 jit_solution(8629027694497266303)
XLA Ops:
  0.6 74.3 %up_backward.1 = (bf16[128,1024]{1,0:T(8,128)(2,1)S(1)}, bf16[1024,1664]{1,0:T(8,128)(2,1)S(1)}) custom-call(bf16[128,1024]{1,0:T(8,128)(2,1)} %act.1, bf16[128,1664]{1,0:T(8,128)(2,1)} %og.1, bf16[1024,1664]{1,0:T(8,128)(2,1)} %w.1), custom_call_target="tpu_custom_call" | custom-call | flops 13958643712 | bytes 13631488 | tf_op jit(solution)/shard_map/up_backward/pallas_call | solution.py:375
  74.9 2.0 %hand_out.1 = (bf16[128,1024]{1,0:T(8,128)(2,1)}, bf16[1024,1664]{1,0:T(8,128)(2,1)}) custom-call(bf16[128,1024]{1,0:T(8,128)(2,1)S(1)} %get-tuple-element.4.ig, bf16[1024,1664]{1,0:T(8,128)(2,1)S(1)} %get-tuple-element.5.wg), custom_call_target="tpu_custom_call" | custom-call | tf_op jit(solution)/shard_map/hand_out/pallas_call | solution.py:403

commit v5 on v4

--- a/solution.py
+++ b/solution.py
@@ -234,12 +234,12 @@
                     top = jnp.maximum(top, jnp.abs(v))
                 return top
 
-            top = lax.fori_loop(0, TB // 16, body, jnp.zeros((16, 128), F32))
+            top = lax.fori_loop(0, TB // 16, body, jnp.zeros((16, 128), F32), unroll=TB // 16)
             scale = jnp.maximum(top * 1.01, 1e-30).astype(BF16)
             CS[u, KC:KC + SCR, :] = scale
             mul = (2 * REACH) / scale.astype(F32)
 
-            @pl.loop(0, TB // 16)
+            @pl.loop(0, TB // 16, unroll=TB // 16)
             def _(i):
                 rr = pl.ds(pl.multiple_of(i * 16, 16), 16)
                 for c in range(DH // 128):
@@ -255,7 +255,7 @@
             for half in range(2):
                 @pl.when(h == half)
                 def _():
-                    @pl.loop(0, TB // 16)
+                    @pl.loop(0, TB // 16, unroll=TB // 16)
                     def _(i):
                         rr = pl.ds(pl.multiple_of(i * 16, 16), 16)
                         for c in range(DH // 128):

time: 78.2 us -> 76.3 us (0.976)
  Pallas kernels: 76.3 us -> 74.6 us
    pallas_call x1, Pallas kernels: 74.3 us -> 72.6 us  [per_device(): pl.pallas_call(kernel, name='up_backward', out_shape=(vmem((TB, DF), BF16...]
where the time goes in v5:
time: 76.3 us; the launch traced here: 75.4 us
  Pallas kernels  74.6 us (98%)
  between operations  0.82 us (1%)
    pallas_call x1, Pallas kernels, per_device(): pl.pallas_call(kernel, name='up_backward', out_shape=(vmem((TB, DF), BF16...  72.6 us
    pallas_call x1, Pallas kernels, per_device(): pl.pallas_call(hand_out, name='hand_out', out_shape=(jax.ShapeDtypeStruct...  1.98 us

profile of v5, /device:TPU:28, one launch (start us, length us, event | category | flops | bytes accessed | tf_op | source)
XLA Modules:
  0.0 75.4 jit_solution(8231920880320369204)
XLA Ops:
  0.6 72.6 %up_backward.1 = (bf16[128,1024]{1,0:T(8,128)(2,1)S(1)}, bf16[1024,1664]{1,0:T(8,128)(2,1)S(1)}) custom-call(bf16[128,1024]{1,0:T(8,128)(2,1)} %act.1, bf16[128,1664]{1,0:T(8,128)(2,1)} %og.1, bf16[1024,1664]{1,0:T(8,128)(2,1)} %w.1), custom_call_target="tpu_custom_call" | custom-call | flops 13958643712 | bytes 13631488 | tf_op jit(solution)/shard_map/up_backward/pallas_call | solution.py:375
  73.3 2.0 %hand_out.1 = (bf16[128,1024]{1,0:T(8,128)(2,1)}, bf16[1024,1664]{1,0:T(8,128)(2,1)}) custom-call(bf16[128,1024]{1,0:T(8,128)(2,1)S(1)} %get-tuple-element.4.ig, bf16[1024,1664]{1,0:T(8,128)(2,1)S(1)} %get-tuple-element.5.wg), custom_call_target="tpu_custom_call" | custom-call | tf_op jit(solution)/shard_map/hand_out/pallas_call | solution.py:403
